TPU v7x, 256 devices: a whole 4x4x8 slice. The times are simulated.
256 devices in a mesh: rep: 8 (over z_hi, core), fsdp: 32 (over y, z_lo, x).
Axes of the slice: x: 4, y: 4, z: 8 (z_hi: 4, z_lo: 2; z = z_hi * 2 + z_lo), core: 2. Of those that a mesh axis runs over, the one named last changes fastest.
Arguments:
- tokens: bfloat16 [8, 8192, 4608], P('rep', 'fsdp'), may hold values from -800 to 800
- norm_scale: float32 [8, 4608], P('rep'), may hold values from 0.25 to 1.75
- value_weight: bfloat16 [8, 4608, 1024], P('rep', 'fsdp'), may hold values from -0.09375 to 0.09375
- cotangent: bfloat16 [8, 8192, 1024], P('rep', 'fsdp'), may hold values from -6 to 6
- replica_weights: bfloat16 [8, 2, 4608, 1024], P('rep', None, 'fsdp'), may hold values from -6 to 6
- base: float32 [2, 4608, 1024], P(None, 'fsdp'), may hold values from -6 to 6
- momentum: float32 [2, 4608, 1024], P(None, 'fsdp'), may hold values from -4 to 4
- fragment: int32 [576], P('fsdp'), may hold values from 0 to 1
Outputs:
- values: bfloat16 [8, 8192, 1024], P('rep', 'fsdp')
- input_grad: bfloat16 [8, 8192, 4608], P('rep', 'fsdp')
- weight_grad: float32 [8, 4608, 1024], P('rep', 'fsdp')
- scale_grad: float32 [8, 4608], P('rep', 'fsdp')
- new_base: float32 [4608, 1024], P('fsdp')
- new_momentum: float32 [4608, 1024], P('fsdp')
All inputs are finite; a program needn't handle non-finite values.
Results may differ from a plain program's by a relative error of at most 0.0049.
Values may be sent and summed in bfloat16 or wider, within the bound.
No kernel may reach another device: no remote copies, remote signals or barrier semaphores. Data moves between devices by JAX's collectives and lax.ppermute only.
A program may use at most 128 MiB of HBM per device.

v0:
```python
import math

import jax
import jax.numpy as jnp
from jax import lax
from jax.sharding import PartitionSpec as P


def inner_step(tokens, norm_scale, value_weight, cotangent):
    inputs = tokens[0].astype(jnp.float32)
    scale_one = norm_scale[0]
    cot_one = cotangent[0]
    weights = value_weight[0]
    inverse = lax.rsqrt(jnp.mean(inputs * inputs, axis=-1, keepdims=True) + 1e-06)
    normed = (inputs * inverse * scale_one).astype(jnp.bfloat16)
    whole = lax.all_gather(weights, "fsdp", axis=0, tiled=True)
    values = jnp.dot(normed, whole, preferred_element_type=jnp.float32)
    back = lax.dot_general(
        cot_one, whole, (((1,), (1,)), ((), ())), preferred_element_type=jnp.float32
    )
    scaled_back = back * scale_one
    input_grad = inverse * (
        scaled_back
        - inputs * (inverse * inverse) * jnp.mean(scaled_back * inputs, axis=-1, keepdims=True)
    )
    scale_part = jnp.sum(back * inputs * inverse, axis=0)
    weight_part = lax.dot_general(
        normed, cot_one, (((0,), (0,)), ((), ())), preferred_element_type=jnp.float32
    )
    weight_sum, scale_sum = (
        lax.psum_scatter(weight_part, "fsdp", scatter_dimension=0, tiled=True),
        lax.psum_scatter(scale_part, "fsdp", scatter_dimension=0, tiled=True),
    )
    factor = 1.0 / math.sqrt(tokens.shape[1] * lax.axis_size("fsdp"))
    return (
        values.astype(jnp.bfloat16)[None],
        input_grad.astype(jnp.bfloat16)[None],
        (weight_sum * factor)[None],
        (scale_sum * factor)[None],
    )


def pick_rows(stack, row_frag):
    result = stack[0]
    result = jnp.where(row_frag[:, None] == 1, stack[1], result)
    return result


def nesterov(pseudo_all, base_rows, moment_rows):
    replicas = pseudo_all.shape[0]
    delta = jnp.sum(pseudo_all.astype(jnp.float32), axis=0) / replicas
    new_momentum = 0.9 * moment_rows + delta
    new_base = base_rows + 0.7 * (delta + 0.9 * new_momentum)
    return (new_base, new_momentum)


def outer_sync(replica_weights, base, momentum, fragment):
    row_frag = jnp.repeat(fragment, 8)
    weights_now = pick_rows(replica_weights[0], row_frag).astype(jnp.float32)
    base_now = pick_rows(base, row_frag)
    moment = pick_rows(momentum, row_frag)
    pseudo = (weights_now - base_now).astype(jnp.bfloat16)
    all_pseudo = lax.all_gather(pseudo[None], "rep", axis=0, tiled=True)
    new_base, new_momentum = nesterov(all_pseudo, base_now, moment)
    return (new_base, new_momentum)


def per_device(
    tokens, norm_scale, value_weight, cotangent, replica_weights, base, momentum, fragment
):
    values, input_grad, weight_grad, scale_grad = inner_step(
        tokens, norm_scale, value_weight, cotangent
    )
    new_base, new_momentum = outer_sync(replica_weights, base, momentum, fragment)
    return (values, input_grad, weight_grad, scale_grad, new_base, new_momentum)


def solution(mesh):
    in_specs = (
        P("rep", "fsdp", None),
        P("rep", None),
        P("rep", "fsdp", None),
        P("rep", "fsdp", None),
        P("rep", None, "fsdp", None),
        P(None, "fsdp", None),
        P(None, "fsdp", None),
        P("fsdp"),
    )
    out_specs = (
        P("rep", "fsdp", None),
        P("rep", "fsdp", None),
        P("rep", "fsdp", None),
        P("rep", "fsdp"),
        P("fsdp", None),
        P("fsdp", None),
    )
    return jax.shard_map(
        per_device, mesh=mesh, in_specs=in_specs, out_specs=out_specs, check_vma=False
    )
```

profile of v0, /device:TPU:64, one launch (start us, length us, event | category | flops | bytes accessed | tf_op | source)
XLA Modules:
  0.0 451.0 jit_solution(11553803169438311596)
XLA Ops:
  7.2 0.0 copy-start
  7.2 0.0 copy-start.1
  7.2 0.0 all-gather.4.cloned.1.call-start
  7.2 0.8 broadcast_compare_fusion
  8.1 0.1 broadcast_in_dim.41
  8.1 0.1 eq.15
  8.2 2.3 subtract_convert_fusion
  10.5 0.0 all-gather.4.cloned.1.call-update
  10.6 0.0 all-gather.6.cloned.1.call-start
  10.6 0.7 all-gather.6.cloned.1.call-update
  11.3 0.0 reduce-scatter.2.cloned.1.call-start
  11.4 0.8 reduce
  12.1 2.2 fusion.9
  14.4 0.0 copy-done
  14.4 0.0 copy-done.1
  14.4 8.0 %fusion.22 = f32[4608,1024]{1,0:T(8,128)} fusion(bf16[1,256,4608]{2,1,0:T(8,128)(2,1)S(1)} %copy-done.1, f32[4608]{0:T(1024)S(1)} %reduce, f32[256]{0:T(256)S(1)} %get-tuple-element.11, bf16[1,256,1024]{2,1,0:T(8,128)(2,1)S(1)} %copy-done), kind=kOutput, calls=%fused_computation.25 | convolution fusion | flops 2420637696 | bytes 21777408 | tf_op jit(solution)/shard_map/dot_general | solution.py:27
  22.4 0.0 copy-start.3
  22.4 0.0 reduce-scatter.2.cloned.1.call-update
  22.4 0.6 copy-done.3
  23.1 0.6 dynamic-slice
  24.3 26.3 %all-gather.4.cloned.1.call-done = bf16[8,144,1024]{2,1,0:T(8,128)(2,1)} async-done(((bf16[1,144,1024]{2,1,0:T(8,128)(2,1)}), bf16[8,144,1024]{2,1,0:T(8,128)(2,1)}) %all-gather.4.cloned.1.call-update) | async-done | bytes 2359312 | tf_op jit(solution)/shard_map/all_gather | solution.py:63
  50.6 2.2 convert_reduce_fusion
  52.8 2.9 fusion.42
  55.7 167.5 %all-gather.6.cloned.1.call-done = bf16[1,4608,1024]{2,1,0:T(8,128)(2,1)} async-done(((bf16[1,144,1024]{2,1,0:T(8,128)(2,1)}), bf16[1,4608,1024]{2,1,0:T(8,128)(2,1)}) %all-gather.6.cloned.1.call-update) | async-done | bytes 9437200 | tf_op jit(solution)/shard_map/all_gather | solution.py:16
  223.2 9.2 %fusion.18 = (f32[4608]{0:T(1024)S(1)}, f32[256]{0:T(256)S(1)}, f32[256,4608]{1,0:T(8,128)}) fusion(bf16[1,256,4608]{2,1,0:T(8,128)(2,1)S(1)} %copy-done.1, f32[256]{0:T(256)S(1)} %get-tuple-element.11, f32[4608]{0:T(1024)S(1)} %reduce, bf16[1,4608,1024]{2,1,0:T(8,128)(2,1)} %all-gather.6.cloned.1.call-done, bf16[1,256,1024]{2,1,0:T(8,128)(2,1)S(1)} %copy-done), kind=kOutput, calls=%fused_computation.20 | convolution fusion | flops 2424171776 | bytes 17078272 | tf_op jit(solution)/shard_map/dot_general | solution.py:18
  232.5 162.4 %all-reduce = f32[4608]{0:T(1024)S(1)} all-reduce(f32[4608]{0:T(1024)S(1)} %get-tuple-element.6), channel_id=4, replica_groups=mesh['rep'=8,'fsdp'=32] {'fsdp'}, use_global_device_ids=true, to_apply=%region_4.0.clone | all-reduce | flops 4608 | bytes 36864
  394.8 0.6 dynamic-slice_multiply_fusion
  395.5 7.4 %fusion.35 = bf16[1,256,1024]{2,1,0:T(8,128)(2,1)} fusion(bf16[1,4608,1024]{2,1,0:T(8,128)(2,1)} %all-gather.6.cloned.1.call-done, bf16[1,256,4608]{2,1,0:T(8,128)(2,1)S(1)} %copy-done.1, f32[4608]{0:T(1024)S(1)} %reduce, f32[256]{0:T(256)S(1)} %get-tuple-element.11), kind=kOutput, calls=%fused_computation.32 | convolution fusion | flops 2420899840 | bytes 12340224 | tf_op jit(solution)/shard_map/dot_general | solution.py:17
  402.8 0.0 copy-done.2
  402.8 3.0 fusion.24
  405.9 36.7 %reduce-scatter.2.cloned.1.call-done = f32[144,1024]{1,0:T(8,128)} async-done(((f32[4608,1024]{1,0:T(8,128)}), f32[144,1024]{1,0:T(8,128)}) %reduce-scatter.2.cloned.1.call-update) | async-done | bytes 589840 | tf_op jit(solution)/shard_map/reduce_scatter | solution.py:31
  442.5 1.9 multiply_bitcast_fusion
  (3 shorter events, 0.0 us)
Async XLA Ops:
  7.2 7.2 %copy-start = (bf16[1,256,1024]{2,1,0:T(8,128)(2,1)S(1)}, bf16[1,256,1024]{2,1,0:T(8,128)(2,1)}, u32[]{:S(2)}) copy-start(bf16[1,256,1024]{2,1,0:T(8,128)(2,1)} %param.11) | copy-start | bytes 1572868
  7.2 7.2 %copy-start.1 = (bf16[1,256,4608]{2,1,0:T(8,128)(2,1)S(1)}, bf16[1,256,4608]{2,1,0:T(8,128)(2,1)}, u32[]{:S(2)}) copy-start(bf16[1,256,4608]{2,1,0:T(8,128)(2,1)} %param.8) | copy-start | bytes 7077892
  7.2 43.4 %all-gather.4.cloned.1.call-start = ((), (), s32[]{:S(2)}) async-start(), calls=%async_computation.2 | async-start | bytes 2654208 | tf_op jit(solution)/shard_map/all_gather | solution.py:63
  10.6 212.7 %all-gather.6.cloned.1.call-start = ((), (), s32[]{:S(2)}) async-start(), calls=%async_computation.3 | async-start | bytes 9732096 | tf_op jit(solution)/shard_map/all_gather | solution.py:16
  11.3 431.2 %reduce-scatter.2.cloned.1.call-start = ((), (), s32[]{:S(2)}) async-start(), calls=%async_computation.1 | async-start | bytes 19464192 | tf_op jit(solution)/shard_map/reduce_scatter | solution.py:31
  22.4 0.7 copy-start.3
  395.5 7.4 %copy-start.2 = (f32[256,4608]{1,0:T(8,128)S(1)}, f32[256,4608]{1,0:T(8,128)}, u32[]{:S(2)}) copy-start(f32[256,4608]{1,0:T(8,128)} %get-tuple-element.12) | copy-start | bytes 14155780
Sparse Core Ops, SparseCore 0:
  10.7 39.9 all-gather.3
  52.4 170.7 all-gather.5
  225.8 216.6 reduce-scatter.1
where the time goes:
time: 453 us; the launch traced here: 451 us
  waiting for transfers between devices  231 us (51%)
  blocking collectives  162 us (36%)
  matrix products  24.6 us (5%)
  other arithmetic  16.8 us (4%)
  between operations  14.4 us (3%)
    all_gather x1, waiting for transfers between devices, inner_step(): whole = lax.all_gather(weights, 'fsdp', axis=0, tiled=True)  168 us
    unnamed x1, blocking collectives  162 us
    reduce_scatter x1, waiting for transfers between devices, inner_step(): lax.psum_scatter(weight_part, 'fsdp', scatter_dimension=0, tiled=True)  36.7 us
    all_gather x1, waiting for transfers between devices, outer_sync(): all_pseudo = lax.all_gather(pseudo[None], 'rep', axis=0, tiled=True)  26.3 us
    dot_general x1, matrix products, inner_step(): lax.dot_general(cot_one, whole, (((1,), (1,)), ((), ())), preferred_eleme...  9.23 us
  transfers between devices with their start and end apart: 3, of which 3 were waited for; matrix products, arithmetic and copies ran while one was open for 8% of the time, Pallas kernels for 0%

commit v1 on v0

v1 whole, which is shorter than its diff:
```python
import functools
import math

import jax
import jax.numpy as jnp
from jax import lax
from jax.experimental import pallas as pl
from jax.experimental.pallas import tpu as pltpu
from jax.sharding import PartitionSpec as P

D = 4608
HV = 1024
ROWS = 144
HALF = D // 2
TOK = 256
NX, NY, NZ = 4, 4, 2
F32, BF16 = jnp.float32, jnp.bfloat16


def fsdp_perm(move):
    pairs = []
    for y in range(NY):
        for z in range(NZ):
            for x in range(NX):
                a, b, c = move(y, z, x)
                pairs.append(((y * NZ + z) * NX + x, (a % NY * NZ + b % NZ) * NX + c % NX))
    return pairs


def after(v, *others):
    return lax.optimization_barrier((v, *others))[0]


def send_x(v, d):
    return lax.ppermute(v, "fsdp", fsdp_perm(lambda y, z, x: (y, z, x + d)))


def send_y(v, d):
    return lax.ppermute(v, "fsdp", fsdp_perm(lambda y, z, x: (y + d, z, x)))


def send_z(v):
    return lax.ppermute(v, "fsdp", fsdp_perm(lambda y, z, x: (y, z + 1, x)))


def send_core(v):
    return lax.ppermute(v, "rep", [(i, i ^ 1) for i in range(8)])


def send_zhi(v, d):
    return lax.ppermute(v, "rep", [(2 * h + c, (h + d) % 4 * 2 + c) for h in range(4) for c in range(2)])


def norm_kernel(where_ref, tok_ref, scale_ref, keep_ref, send_ref, turned):
    y, z, x = where_ref[0], where_ref[1], where_ref[2]
    total = jnp.zeros((TOK, 128), F32)
    for k in range(D // 128):
        part = tok_ref[:, k * 128 : (k + 1) * 128].astype(F32)
        total = total + part * part
    inverse = lax.rsqrt(jnp.sum(total, axis=1, keepdims=True) * (1.0 / D) + 1e-06)
    for k in range(D // 128):
        cols = slice(k * 128, (k + 1) * 128)
        part = tok_ref[:, cols].astype(F32) * inverse * scale_ref[:, cols]
        turned[cols, :] = part.T.astype(BF16)
    for dy in range(NY):
        for dx in range(NX):
            at = slice((dy * NX + dx) * ROWS, (dy * NX + dx + 1) * ROWS)
            row, col = lax.rem(y + dy, NY), lax.rem(x + dx, NX)
            for out, side in ((keep_ref, z), (send_ref, 1 - z)):
                start = pl.multiple_of(((row * NZ + side) * NX + col) * ROWS, 16)
                out[at, :] = turned[pl.ds(start, ROWS), :]


def norm_turned(where, tokens, scale):
    vmem = pl.BlockSpec(memory_space=pltpu.VMEM)
    return pl.pallas_call(
        norm_kernel,
        out_shape=[
            jax.ShapeDtypeStruct((HALF, TOK), BF16),
            jax.ShapeDtypeStruct((HALF, TOK), BF16),
        ],
        in_specs=[pl.BlockSpec(memory_space=pltpu.SMEM), vmem, vmem],
        out_specs=[vmem] * 2,
        scratch_shapes=[pltpu.VMEM((D, TOK), BF16)],
        compiler_params=pltpu.CompilerParams(vmem_limit_bytes=32 << 20),
        cost_estimate=pl.CostEstimate(flops=8 * TOK * D, bytes_accessed=16 << 20, transcendentals=256),
        name="norm",
    )(where, tokens, scale)


def grad_kernel(keep_ref, got_ref, cot_ref, other_ref, low_ref, high_ref):
    for out, cols in ((low_ref, slice(0, HV // 2)), (high_ref, slice(HV // 2, HV))):
        part = jnp.dot(keep_ref[...], cot_ref[:, cols], preferred_element_type=F32)
        part = part + jnp.dot(got_ref[...], other_ref[:, cols], preferred_element_type=F32)
        out[...] = part.astype(BF16)


def grad_terms(keep, got, cot, other):
    tile = 288
    rows = pl.BlockSpec((tile, TOK), lambda i: (i, 0))
    whole = pl.BlockSpec((TOK, HV), lambda i: (0, 0))
    out = pl.BlockSpec((tile, HV // 2), lambda i: (i, 0))
    return pl.pallas_call(
        grad_kernel,
        grid=(HALF // tile,),
        out_shape=[jax.ShapeDtypeStruct((HALF, HV // 2), BF16)] * 2,
        in_specs=[rows, rows, whole, whole],
        out_specs=[out, out],
        compiler_params=pltpu.CompilerParams(vmem_limit_bytes=32 << 20),
        cost_estimate=pl.CostEstimate(
            flops=2 * HALF * 2 * TOK * HV, bytes_accessed=10 << 20, transcendentals=0
        ),
        name="weight_terms",
    )(keep, got, cot, other)


PIECES = ((0, (0, 1, 2, 3)), (3, (0, 1, 2, 3)), (1, (0, 1, 2, 3)), (2, (0, 1)), (2, (2, 3)))
N_PIECES = 2 * len(PIECES)


def model_kernel(*refs):
    where_ref, tok_ref, scale_ref, cot_ref = refs[:4]
    pieces = refs[4 : 4 + N_PIECES]
    val_ref, grad_ref = refs[4 + N_PIECES : 6 + N_PIECES]
    whole, normed, back, sems = refs[6 + N_PIECES :]
    y, z, x = where_ref[0], where_ref[1], where_ref[2]
    copies = []
    for half in range(2):
        for n, (ring, line) in enumerate(PIECES):
            ref = pieces[half * len(PIECES) + n]
            for i, d in enumerate(line):
                for side in range(2):
                    if half == 0:
                        row, col = lax.rem(y + ring, NY), lax.rem(x + d, NX)
                    else:
                        row, col = lax.rem(y + d, NY), lax.rem(x + ring, NX)
                    zc = z if side == 0 else 1 - z
                    at = pl.multiple_of(((row * NZ + zc) * NX + col) * ROWS, 16)
                    copy = pltpu.make_async_copy(
                        ref.at[i, side],
                        whole.at[pl.ds(at, ROWS), pl.ds(half * 512, 512)],
                        sems.at[len(copies)],
                    )
                    copy.start()
                    copies.append(copy)
    total = jnp.zeros((TOK, 128), F32)
    for k in range(D // 128):
        part = tok_ref[:, k * 128 : (k + 1) * 128].astype(F32)
        total = total + part * part
    inverse = lax.rsqrt(jnp.sum(total, axis=1, keepdims=True) * (1.0 / D) + 1e-06)
    for k in range(D // 256):
        cols = slice(k * 256, (k + 1) * 256)
        part = tok_ref[:, cols].astype(F32) * inverse * scale_ref[:, cols]
        normed[:, cols] = part.astype(BF16)
    for copy in copies:
        copy.wait()

    def project(i, _):
        cols = pl.ds(pl.multiple_of(i * 256, 256), 256)
        val_ref[:, cols] = jnp.dot(normed[...], whole[:, cols], preferred_element_type=F32).astype(BF16)
        return 0

    lax.fori_loop(0, HV // 256, project, 0)

    def pull(i, sums):
        at = pl.ds(pl.multiple_of(i * 256, 256), 256)
        term = lax.dot_general(
            cot_ref[...], whole[at, :], (((1,), (1,)), ((), ())), preferred_element_type=F32
        )
        toks = tok_ref[:, at].astype(F32)
        back[:, at] = term
        mixed = term * scale_ref[:, at] * toks
        return sums + mixed[:, :128] + mixed[:, 128:]

    sums = lax.fori_loop(0, D // 256, pull, jnp.zeros((TOK, 128), F32))
    mean = jnp.sum(sums, axis=1, keepdims=True) * (1.0 / D)
    lean = inverse * inverse * mean

    def finish(i, _):
        at = pl.ds(pl.multiple_of(i * 256, 256), 256)
        grad = inverse * (back[:, at] * scale_ref[:, at] - tok_ref[:, at].astype(F32) * lean)
        grad_ref[:, at] = grad.astype(BF16)
        return 0

    lax.fori_loop(0, D // 256, finish, 0)


def model_step(where, tokens, scale, cot, pieces):
    vmem = pl.BlockSpec(memory_space=pltpu.VMEM)
    return pl.pallas_call(
        model_kernel,
        out_shape=[
            jax.ShapeDtypeStruct((TOK, HV), BF16),
            jax.ShapeDtypeStruct((TOK, D), BF16),
        ],
        in_specs=[pl.BlockSpec(memory_space=pltpu.SMEM), vmem, vmem, vmem]
        + [pl.BlockSpec(memory_space=pl.ANY)] * N_PIECES,
        out_specs=[vmem, vmem],
        scratch_shapes=[
            pltpu.VMEM((D, HV), BF16),
            pltpu.VMEM((TOK, D), BF16),
            pltpu.VMEM((TOK, D), F32),
            pltpu.SemaphoreType.DMA((64,)),
        ],
        compiler_params=pltpu.CompilerParams(vmem_limit_bytes=48 << 20),
        cost_estimate=pl.CostEstimate(
            flops=4 * TOK * D * HV, bytes_accessed=32 << 20, transcendentals=256
        ),
        name="model_step",
    )(where, tokens, scale, cot, *pieces)


def gather_half(pair, first, second):
    near = jnp.stack([pair, first(pair, -1), first(pair, 2), first(pair, 1)])
    left, right = second(near, 1), second(near, -1)
    return [near, left, right, second(left[:2], 1), second(right[2:], -1)]


def ring_sum(blocks, send):
    n = blocks[0].shape[0] // 2
    to_far, back_far = send(blocks[2][:n], 1), send(blocks[2][n:], -1)
    up = jnp.concatenate([(blocks[1][:n].astype(F32) + to_far.astype(F32)).astype(BF16), blocks[1][n:]])
    down = jnp.concatenate([blocks[3][:n], (blocks[3][n:].astype(F32) + back_far.astype(F32)).astype(BF16)])
    return blocks[0].astype(F32) + send(up, 1).astype(F32) + send(down, -1).astype(F32)


def direct_sum(blocks, send):
    return (
        blocks[0].astype(F32)
        + send(blocks[1].astype(BF16), 1).astype(F32)
        + send(blocks[3].astype(BF16), -1).astype(F32)
        + send(blocks[2].astype(BF16), 2).astype(F32)
    )


def scatter_sum_half(terms, second_first, first):
    return direct_sum(list(ring_sum([terms[d] for d in range(4)], second_first)), first)


def pick(stack, row_frag):
    return jnp.where(row_frag[:, None] == 1, stack[1], stack[0])


def outer_sync(replica_weights, base, momentum, fragment, wait):
    row_frag = jnp.repeat(fragment, 8)
    base_now = pick(base, row_frag)
    moment = pick(momentum, row_frag)
    pseudo = (pick(replica_weights[0], row_frag).astype(F32) - base_now).astype(BF16)
    everyone = lax.all_gather(after(pseudo, wait), "rep", axis=0)
    delta = jnp.sum(everyone.astype(F32), axis=0) / everyone.shape[0]
    new_momentum = 0.9 * moment + delta
    new_base = base_now + 0.7 * (delta + 0.9 * new_momentum)
    return new_base, new_momentum


def per_device(
    tokens, norm_scale, value_weight, cotangent, replica_weights, base, momentum, fragment
):
    tokens, weight, cot = tokens[0], value_weight[0], cotangent[0]
    me = lax.axis_index("fsdp")
    where = jnp.stack([me // (NZ * NX), me // NX % NZ, me % NX]).astype(jnp.int32)
    other_weight = send_z(weight)
    keep, give = norm_turned(where, tokens, norm_scale)
    partner_cot = send_z(after(cot, other_weight, give))
    got = send_z(after(give, partner_cot))
    pieces = []
    for half in range(2):
        order = (send_x, send_y) if half == 0 else (send_y, send_x)
        cols = slice(half * 512, half * 512 + 512)
        pieces += gather_half(jnp.stack([weight[:, cols], other_weight[:, cols]]), *order)
    low, high = grad_terms(keep, got, cot, partner_cot)
    low = low.reshape(NY, NX, ROWS, HV // 2)
    high = high.reshape(NY, NX, ROWS, HV // 2).swapaxes(0, 1)
    factor = 1.0 / math.sqrt(TOK * NX * NY * NZ)
    weight_grad = jnp.concatenate(
        [scatter_sum_half(low, send_y, send_x), scatter_sum_half(high, send_x, send_y)], axis=1
    ) * factor
    mine = lax.dynamic_slice_in_dim(norm_scale[0], me * ROWS, ROWS)
    scale_grad = jnp.sum(weight.astype(F32) * weight_grad, axis=1) / mine
    values, input_grad = model_step(where, tokens, norm_scale, cot, pieces)
    new_base, new_momentum = outer_sync(replica_weights, base, momentum, fragment, got)
    return (
        values[None],
        input_grad[None],
        weight_grad[None],
        scale_grad[None],
        new_base,
        new_momentum,
    )


def solution(mesh):
    in_specs = (
        P("rep", "fsdp", None),
        P("rep", None),
        P("rep", "fsdp", None),
        P("rep", "fsdp", None),
        P("rep", None, "fsdp", None),
        P(None, "fsdp", None),
        P(None, "fsdp", None),
        P("fsdp"),
    )
    out_specs = (
        P("rep", "fsdp", None),
        P("rep", "fsdp", None),
        P("rep", "fsdp", None),
        P("rep", "fsdp"),
        P("fsdp", None),
        P("fsdp", None),
    )
    return jax.shard_map(
        per_device, mesh=mesh, in_specs=in_specs, out_specs=out_specs, check_vma=False
    )
```

time: 453 us -> 149 us (0.33)
  waiting for transfers between devices: 231 us -> 37.1 us
  blocking collectives: 162 us -> 0 us
  starting transfers between devices: 0.12 us -> 43.9 us
  matrix products: 24.6 us -> 0 us
  Pallas kernels: 0 us -> 23.1 us
  local copies, waits for them, and re-layouts: 1.42 us -> 17.2 us
    all_gather x2 -> x1, waiting for transfers between devices: 194 us -> 0.01 us  [outer_sync(): everyone = lax.all_gather(after(pseudo, wait), 'rep', axis=0)]
    unnamed x1 -> x0, blocking collectives: 162 us -> none
    ppermute x0 -> x31, starting transfers between devices: none -> 43.9 us  [the longest x14 19.7 us: send_x(): return lax.ppermute(v, 'fsdp', fsdp_perm(lambda y, z, x: (y, z, x + d)))]
    ppermute x0 -> x31, waiting for transfers between devices: none -> 37.1 us  [the longest x14 23.4 us: send_y(): return lax.ppermute(v, 'fsdp', fsdp_perm(lambda y, z, x: (y + d, z, x)))]
    reduce_scatter x1 -> x0, waiting for transfers between devices: 36.7 us -> none  [inner_step(): lax.psum_scatter(weight_part, 'fsdp', scatter_dimension=0, tiled=True)]
    dot_general x3 -> x0, matrix products: 24.6 us -> none  [the longest x1 9.23 us: inner_step(): lax.dot_general(cot_one, whole, (((1,), (1,)), ((), ())), preferred_eleme...]
    pallas_call x0 -> x3, Pallas kernels: none -> 23.1 us  [the longest x1 17.3 us: model_step(): pl.pallas_call(model_kernel, out_shape=[jax.ShapeDtypeStruct((TOK, HV), B...]
    unnamed x9 -> x52, local copies, waits for them, and re-layouts: 1.25 us -> 9.57 us
  transfers between devices with their start and end apart: 3 -> 32, of which waited for: 3 -> 13; matrix products, arithmetic and copies ran while one was open for 8% -> 11% of each run, Pallas kernels for 0% -> 16%
where the time goes in v1:
time: 149 us; the launch traced here: 148 us
  starting transfers between devices  43.9 us (29%)
  waiting for transfers between devices  37.1 us (25%)
  Pallas kernels  23.1 us (16%)
  local copies, waits for them, and re-layouts  17.2 us (12%)
  between operations  14.4 us (10%)
  other arithmetic  12.3 us (8%)
    ppermute x14, waiting for transfers between devices, send_y(): return lax.ppermute(v, 'fsdp', fsdp_perm(lambda y, z, x: (y + d, z, x)))  23.4 us
    ppermute x14, starting transfers between devices, send_x(): return lax.ppermute(v, 'fsdp', fsdp_perm(lambda y, z, x: (y, z, x + d)))  19.7 us
    ppermute x14, starting transfers between devices, send_y(): return lax.ppermute(v, 'fsdp', fsdp_perm(lambda y, z, x: (y + d, z, x)))  18.9 us
    pallas_call x1, Pallas kernels, model_step(): pl.pallas_call(model_kernel, out_shape=[jax.ShapeDtypeStruct((TOK, HV), B...  17.3 us
    ppermute x3, waiting for transfers between devices, send_z(): return lax.ppermute(v, 'fsdp', fsdp_perm(lambda y, z, x: (y, z + 1, x)))  9.59 us
    unnamed x52, local copies, waits for them, and re-layouts  9.57 us
    ppermute x3, starting transfers between devices, send_z(): return lax.ppermute(v, 'fsdp', fsdp_perm(lambda y, z, x: (y, z + 1, x)))  5.28 us
    slice x4, local copies, waits for them, and re-layouts, gather_half(): return [near, left, right, second(left[:2], 1), second(right[2:], -1)]  4.74 us
  transfers between devices with their start and end apart: 32, of which 13 were waited for; matrix products, arithmetic and copies ran while one was open for 11% of the time, Pallas kernels for 16%

profile of v1, /device:TPU:64, one launch (start us, length us, event | category | flops | bytes accessed | tf_op | source)
XLA Modules:
  0.0 148.0 jit_solution(3649060775957262357)
XLA Ops:
  7.2 2.0 %collective-permute-start = (bf16[144,1024]{1,0:T(8,128)(2,1)}, bf16[144,1024]{1,0:T(8,128)(2,1)S(1)}, u32[]{:S(2)}, u32[]{:S(2)}) collective-permute-start(bf16[144,1024]{1,0:T(8,128)(2,1)} %bitcast.143), channel_id=1, source_target_pairs={{0,4},{1,5},{2,6},{3,7},{4,0},{5,1},{6,2},{7,3},{8,12},{9,13},{10,... | collective-permute-start | bytes 884744 | tf_op jit(solution)/shard_map/ppermute | solution.py:43
  9.3 1.7 %copy-done = bf16[1,256,4608]{2,1,0:T(8,128)(2,1)S(1)} copy-done((bf16[1,256,4608]{2,1,0:T(8,128)(2,1)S(1)}, bf16[1,256,4608]{2,1,0:T(8,128)(2,1)}, u32[]{:S(2)}) %copy-start) | copy-done | bytes 2359320
  11.7 2.0 %norm.1 = (bf16[2304,256]{1,0:T(8,128)(2,1)S(1)}, bf16[2304,256]{1,0:T(8,128)(2,1)S(1)}) custom-call(s32[3]{0:T(128)S(1)} %pad_add_fusion.refs_0_.where_ref, bf16[256,4608]{1,0:T(8,128)(2,1)S(1)} %bitcast.127, f32[1,4608]{1,0:T(1,128)S(1)} %copy-done.1), custom_call_target="tpu_custom_call" | custom-call | flops 9437184 | bytes 16777216 | tf_op jit(solution)/shard_map/norm/pallas_call | solution.py:76
  13.7 2.7 %collective-permute-done = bf16[144,1024]{1,0:T(8,128)(2,1)S(1)} collective-permute-done((bf16[144,1024]{1,0:T(8,128)(2,1)}, bf16[144,1024]{1,0:T(8,128)(2,1)S(1)}, u32[]{:S(2)}, u32[]{:S(2)}) %collective-permute-start) | collective-permute-done | bytes 294944 | tf_op jit(solution)/shard_map/ppermute | solution.py:43
  16.4 1.7 %collective-permute-start.15 = (bf16[256,1024]{1,0:T(8,128)(2,1)S(1)}, bf16[256,1024]{1,0:T(8,128)(2,1)S(1)}, u32[]{:S(2)}, u32[]{:S(2)}) collective-permute-start(bf16[256,1024]{1,0:T(8,128)(2,1)S(1)} %bitcast.129), channel_id=1, source_target_pairs={{0,4},{1,5},{2,6},{3,7},{4,0},{5,1},{6,2},{7,3},{8,12},{9,13},{10,... | collective-permute-start | bytes 1572872 | tf_op jit(solution)/shard_map/ppermute | solution.py:43
  18.3 1.6 %collective-permute-start.3 = (bf16[2,144,512]{2,1,0:T(8,128)(2,1)S(1)}, bf16[2,144,512]{2,1,0:T(8,128)(2,1)S(1)}, u32[]{:S(2)}, u32[]{:S(2)}) collective-permute-start(bf16[2,144,512]{2,1,0:T(8,128)(2,1)S(1)} %get-tuple-element.55), channel_id=1, source_target_pairs={{0,1},{1,2},{2,3},{3,0},{4,5},{5,6},{6,7},{7,4},{8,9},{9,10},{10,1... | collective-permute-start | bytes 884744 | tf_op jit(solution)/shard_map/ppermute | solution.py:35
  19.9 2.7 %collective-permute-start.2 = (bf16[2,144,512]{2,1,0:T(8,128)(2,1)S(1)}, bf16[2,144,512]{2,1,0:T(8,128)(2,1)S(1)}, u32[]{:S(2)}, u32[]{:S(2)}) collective-permute-start(bf16[2,144,512]{2,1,0:T(8,128)(2,1)S(1)} %get-tuple-element.55), channel_id=1, source_target_pairs={{0,2},{1,3},{2,0},{3,1},{4,6},{5,7},{6,4},{7,5},{8,10},{9,11},{10,... | collective-permute-start | bytes 884744 | tf_op jit(solution)/shard_map/ppermute | solution.py:35
  22.6 6.9 %collective-permute-done.15.other_ref = bf16[256,1024]{1,0:T(8,128)(2,1)S(1)} collective-permute-done((bf16[256,1024]{1,0:T(8,128)(2,1)S(1)}, bf16[256,1024]{1,0:T(8,128)(2,1)S(1)}, u32[]{:S(2)}, u32[]{:S(2)}) %collective-permute-start.15) | collective-permute-done | bytes 524320 | tf_op jit(solution)/shard_map/ppermute | solution.py:43
  30.2 1.5 %collective-permute-start.16 = (bf16[2304,256]{1,0:T(8,128)(2,1)S(1)}, bf16[2304,256]{1,0:T(8,128)(2,1)S(1)}, u32[]{:S(2)}, u32[]{:S(2)}) collective-permute-start(bf16[2304,256]{1,0:T(8,128)(2,1)S(1)} %get-tuple-element.20), channel_id=1, source_target_pairs={{0,4},{1,5},{2,6},{3,7},{4,0},{5,1},{6,2},{7,3},{8,12},{9,13},{10,... | collective-permute-start | bytes 3538952 | tf_op jit(solution)/shard_map/ppermute | solution.py:43
  31.8 2.8 %collective-permute-start.1 = (bf16[2,144,512]{2,1,0:T(8,128)(2,1)S(1)}, bf16[2,144,512]{2,1,0:T(8,128)(2,1)S(1)}, u32[]{:S(2)}, u32[]{:S(2)}) collective-permute-start(bf16[2,144,512]{2,1,0:T(8,128)(2,1)S(1)} %get-tuple-element.55), channel_id=1, source_target_pairs={{0,3},{1,0},{2,1},{3,2},{4,7},{5,4},{6,5},{7,6},{8,11},{9,8},{10,9... | collective-permute-start | bytes 884744 | tf_op jit(solution)/shard_map/ppermute | solution.py:35
  34.6 1.7 %collective-permute-start.10 = (bf16[2,144,512]{2,1,0:T(8,128)(2,1)S(1)}, bf16[2,144,512]{2,1,0:T(8,128)(2,1)S(1)}, u32[]{:S(2)}, u32[]{:S(2)}) collective-permute-start(bf16[2,144,512]{2,1,0:T(8,128)(2,1)S(1)} %get-tuple-element.49), channel_id=1, source_target_pairs={{0,8},{1,9},{2,10},{3,11},{4,12},{5,13},{6,14},{7,15},{8,16},{9,17... | collective-permute-start | bytes 884744 | tf_op jit(solution)/shard_map/ppermute | solution.py:39
  36.2 2.9 %collective-permute-start.9 = (bf16[2,144,512]{2,1,0:T(8,128)(2,1)S(1)}, bf16[2,144,512]{2,1,0:T(8,128)(2,1)S(1)}, u32[]{:S(2)}, u32[]{:S(2)}) collective-permute-start(bf16[2,144,512]{2,1,0:T(8,128)(2,1)S(1)} %get-tuple-element.49), channel_id=1, source_target_pairs={{0,16},{1,17},{2,18},{3,19},{4,20},{5,21},{6,22},{7,23},{8,24},{9,... | collective-permute-start | bytes 884744 | tf_op jit(solution)/shard_map/ppermute | solution.py:39
  39.1 1.3 collective-permute-start.8
  41.4 7.0 %collective-permute-done.10 = bf16[2,144,512]{2,1,0:T(8,128)(2,1)S(1)} collective-permute-done((bf16[2,144,512]{2,1,0:T(8,128)(2,1)S(1)}, bf16[2,144,512]{2,1,0:T(8,128)(2,1)S(1)}, u32[]{:S(2)}, u32[]{:S(2)}) %collective-permute-start.10) | collective-permute-done | bytes 294944 | tf_op jit(solution)/shard_map/ppermute | solution.py:39
  48.4 5.0 %collective-permute-done.9 = bf16[2,144,512]{2,1,0:T(8,128)(2,1)S(1)} collective-permute-done((bf16[2,144,512]{2,1,0:T(8,128)(2,1)S(1)}, bf16[2,144,512]{2,1,0:T(8,128)(2,1)S(1)}, u32[]{:S(2)}, u32[]{:S(2)}) %collective-permute-start.9) | collective-permute-done | bytes 294944 | tf_op jit(solution)/shard_map/ppermute | solution.py:39
  54.6 3.2 %collective-permute-start.12 = (bf16[4,2,144,512]{3,2,1,0:T(8,128)(2,1)}, bf16[4,2,144,512]{3,2,1,0:T(8,128)(2,1)}, u32[]{:S(2)}, u32[]{:S(2)}) collective-permute-start(bf16[4,2,144,512]{3,2,1,0:T(8,128)(2,1)} %pad_maximum_fusion.1.refs_9_), channel_id=1, source_target_pairs={{0,3},{1,0},{2,1},{3,2},{4,7},{5,4},{6,5},{7,6},{8,11},{9,8},{10,9... | collective-permute-start | bytes 3538952 | tf_op jit(solution)/shard_map/ppermute | solution.py:35
  58.0 2.3 %subtract_convert_fusion = bf16[144,1024]{1,0:T(8,128)(2,1)} fusion(bf16[1,2,144,1024]{3,2,1,0:T(8,128)(2,1)} %param.12, pred[144]{0:T(512)(128)(4,1)S(1)} %eq.18, f32[2,144,1024]{2,1,0:T(8,128)} %param.13), kind=kLoop, calls=%fused_computation.30 | loop fusion | flops 737280 | bytes 2064528 | tf_op jit(solution)/shard_map/convert_element_type | solution.py:248
  66.0 3.8 %weight_terms.1 = (bf16[2304,512]{1,0:T(8,128)(2,1)S(1)}, bf16[2304,512]{1,0:T(8,128)(2,1)S(1)}) custom-call(bf16[2304,256]{1,0:T(8,128)(2,1)S(1)} %copy-done.4, bf16[2304,256]{1,0:T(8,128)(2,1)S(1)} %copy-done.6, bf16[256,1024]{1,0:T(8,128)(2,1)S(1)} %bitcast.130, bf16[256,1024]{1,0:T(8,128)(2,1)S(1)} %copy-done.11), custom_call_target="tpu_custom_call" | custom-call | flops 2415919104 | bytes 10485760 | tf_op jit(solution)/shard_map/weight_terms/pallas_call | solution.py:103
  71.8 2.5 %collective-permute-done.4.refs_5_ = bf16[4,2,144,512]{3,2,1,0:T(8,128)(2,1)} collective-permute-done((bf16[4,2,144,512]{3,2,1,0:T(8,128)(2,1)S(1)}, bf16[4,2,144,512]{3,2,1,0:T(8,128)(2,1)}, u32[]{:S(2)}, u32[]{:S(2)}) %collective-permute-start.4) | collective-permute-done | bytes 1179680 | tf_op jit(solution)/shard_map/ppermute | solution.py:39
  76.4 1.5 collective-permute-start.19
  80.3 3.8 %collective-permute-start.6 = (bf16[2,2,144,512]{3,2,1,0:T(8,128)(2,1)S(1)}, bf16[2,2,144,512]{3,2,1,0:T(8,128)(2,1)S(1)}, u32[]{:S(2)}, u32[]{:S(2)}) collective-permute-start(bf16[2,2,144,512]{3,2,1,0:T(8,128)(2,1)S(1)} %slice.174), channel_id=1, source_target_pairs={{0,8},{1,9},{2,10},{3,11},{4,12},{5,13},{6,14},{7,15},{8,16},{9,17... | collective-permute-start | bytes 1769480 | tf_op jit(solution)/shard_map/ppermute | solution.py:39
  84.1 1.3 slice.178
  87.2 3.0 %collective-permute-start.14 = (bf16[2,2,144,512]{3,2,1,0:T(8,128)(2,1)S(1)}, bf16[2,2,144,512]{3,2,1,0:T(8,128)(2,1)S(1)}, u32[]{:S(2)}, u32[]{:S(2)}) collective-permute-start(bf16[2,2,144,512]{3,2,1,0:T(8,128)(2,1)S(1)} %slice.179), channel_id=1, source_target_pairs={{0,3},{1,0},{2,1},{3,2},{4,7},{5,4},{6,5},{7,6},{8,11},{9,8},{10,9... | collective-permute-start | bytes 1769480 | tf_op jit(solution)/shard_map/ppermute | solution.py:35
  91.4 1.9 %collective-permute-start.17 = (bf16[2,144,512]{2,1,0:T(8,128)(2,1)S(1)}, bf16[2,144,512]{2,1,0:T(8,128)(2,1)S(1)}, u32[]{:S(2)}, u32[]{:S(2)}) collective-permute-start(bf16[2,144,512]{2,1,0:T(8,128)(2,1)S(1)} %bitcast.145), channel_id=1, source_target_pairs={{0,8},{1,9},{2,10},{3,11},{4,12},{5,13},{6,14},{7,15},{8,16},{9,17... | collective-permute-start | bytes 884744 | tf_op jit(solution)/shard_map/ppermute | solution.py:39
  94.5 6.0 %collective-permute-done.17 = bf16[2,144,512]{2,1,0:T(8,128)(2,1)S(1)} collective-permute-done((bf16[2,144,512]{2,1,0:T(8,128)(2,1)S(1)}, bf16[2,144,512]{2,1,0:T(8,128)(2,1)S(1)}, u32[]{:S(2)}, u32[]{:S(2)}) %collective-permute-start.17) | collective-permute-done | bytes 294944 | tf_op jit(solution)/shard_map/ppermute | solution.py:39
  103.0 2.0 %collective-permute-start.18 = (bf16[4,144,512]{2,1,0:T(8,128)(2,1)S(1)}, bf16[4,144,512]{2,1,0:T(8,128)(2,1)S(1)}, u32[]{:S(2)}, u32[]{:S(2)}) collective-permute-start(bf16[4,144,512]{2,1,0:T(8,128)(2,1)S(1)} %pad_maximum_fusion.2), channel_id=1, source_target_pairs={{0,8},{1,9},{2,10},{3,11},{4,12},{5,13},{6,14},{7,15},{8,16},{9,17... | collective-permute-start | bytes 1769480 | tf_op jit(solution)/shard_map/ppermute | solution.py:39
  105.0 17.3 %model_step.1 = (bf16[256,1024]{1,0:T(8,128)(2,1)}, bf16[256,4608]{1,0:T(8,128)(2,1)}) custom-call(s32[3]{0:T(128)S(1)} %pad_add_fusion.refs_0_.where_ref, bf16[256,4608]{1,0:T(8,128)(2,1)} %bitcast.126, f32[1,4608]{1,0:T(1,128)S(1)} %copy-done.2, bf16[256,1024]{1,0:T(8,128)(2,1)S(1)} %bitcast.131, bf16[4,2,144,512]{3,2,1,0:T(8,128)(2,1)S(1)} %pad_maximum_fusion.refs_4_, ...), custom_call_target="tpu_custom_call" | custom-call | flops 4831838208 | bytes 33554432 | tf_op jit(solution)/shard_map/model_step/pallas_call | solution.py:190
  122.9 2.6 %collective-permute-start.29 = (bf16[144,512]{1,0:T(8,128)(2,1)S(1)}, bf16[144,512]{1,0:T(8,128)(2,1)S(1)}, u32[]{:S(2)}, u32[]{:S(2)}) collective-permute-start(bf16[144,512]{1,0:T(8,128)(2,1)S(1)} %get-tuple-element.47), channel_id=1, source_target_pairs={{0,24},{1,25},{2,26},{3,27},{4,28},{5,29},{6,30},{7,31},{8,0},{9,1... | collective-permute-start | bytes 442376 | tf_op jit(solution)/shard_map/ppermute | solution.py:39
  126.8 2.2 %collective-permute-start.22 = (bf16[144,512]{1,0:T(8,128)(2,1)S(1)}, bf16[144,512]{1,0:T(8,128)(2,1)S(1)}, u32[]{:S(2)}, u32[]{:S(2)}) collective-permute-start(bf16[144,512]{1,0:T(8,128)(2,1)S(1)} %get-tuple-element.44), channel_id=1, source_target_pairs={{0,3},{1,0},{2,1},{3,2},{4,7},{5,4},{6,5},{7,6},{8,11},{9,8},{10,9... | collective-permute-start | bytes 442376 | tf_op jit(solution)/shard_map/ppermute | solution.py:35
  129.9 2.1 %collective-permute-done.28 = bf16[144,512]{1,0:T(8,128)(2,1)S(1)} collective-permute-done((bf16[144,512]{1,0:T(8,128)(2,1)S(1)}, bf16[144,512]{1,0:T(8,128)(2,1)S(1)}, u32[]{:S(2)}, u32[]{:S(2)}) %collective-permute-start.28) | collective-permute-done | bytes 147488 | tf_op jit(solution)/shard_map/ppermute | solution.py:39
  133.6 2.2 %collective-permute-done.21 = bf16[144,512]{1,0:T(8,128)(2,1)S(1)} collective-permute-done((bf16[144,512]{1,0:T(8,128)(2,1)S(1)}, bf16[144,512]{1,0:T(8,128)(2,1)S(1)}, u32[]{:S(2)}, u32[]{:S(2)}) %collective-permute-start.21) | collective-permute-done | bytes 147488 | tf_op jit(solution)/shard_map/ppermute | solution.py:35
  137.6 2.3 %convert_reduce_fusion = f32[144,1024]{1,0:T(8,128)S(1)} fusion(bf16[8,144,1024]{2,1,0:T(8,128)(2,1)} %bitcast.138), kind=kLoop, calls=%fused_computation | loop fusion | flops 2211840 | bytes 2949120 | tf_op jit(solution)/shard_map/reduce_sum | solution.py:250
  (125 shorter events, 30.1 us)
Async XLA Ops:
  7.2 130.4 %all-gather.3.cloned.1.call-start = ((), (), s32[]{:S(2)}) async-start(), calls=%async_computation | async-start | bytes 2654208 | tf_op jit(solution)/shard_map/all_gather | solution.py:249
  7.2 9.2 %collective-permute-start = (bf16[144,1024]{1,0:T(8,128)(2,1)}, bf16[144,1024]{1,0:T(8,128)(2,1)S(1)}, u32[]{:S(2)}, u32[]{:S(2)}) collective-permute-start(bf16[144,1024]{1,0:T(8,128)(2,1)} %bitcast.143), channel_id=1, source_target_pairs={{0,4},{1,5},{2,6},{3,7},{4,0},{5,1},{6,2},{7,3},{8,12},{9,13},{10,... | collective-permute-start | bytes 884744 | tf_op jit(solution)/shard_map/ppermute | solution.py:43
  16.4 13.0 %collective-permute-start.15 = (bf16[256,1024]{1,0:T(8,128)(2,1)S(1)}, bf16[256,1024]{1,0:T(8,128)(2,1)S(1)}, u32[]{:S(2)}, u32[]{:S(2)}) collective-permute-start(bf16[256,1024]{1,0:T(8,128)(2,1)S(1)} %bitcast.129), channel_id=1, source_target_pairs={{0,4},{1,5},{2,6},{3,7},{4,0},{5,1},{6,2},{7,3},{8,12},{9,13},{10,... | collective-permute-start | bytes 1572872 | tf_op jit(solution)/shard_map/ppermute | solution.py:43
  18.3 17.9 %collective-permute-start.3 = (bf16[2,144,512]{2,1,0:T(8,128)(2,1)S(1)}, bf16[2,144,512]{2,1,0:T(8,128)(2,1)S(1)}, u32[]{:S(2)}, u32[]{:S(2)}) collective-permute-start(bf16[2,144,512]{2,1,0:T(8,128)(2,1)S(1)} %get-tuple-element.55), channel_id=1, source_target_pairs={{0,1},{1,2},{2,3},{3,0},{4,5},{5,6},{6,7},{7,4},{8,9},{9,10},{10,1... | collective-permute-start | bytes 884744 | tf_op jit(solution)/shard_map/ppermute | solution.py:35
  19.9 19.3 %collective-permute-start.2 = (bf16[2,144,512]{2,1,0:T(8,128)(2,1)S(1)}, bf16[2,144,512]{2,1,0:T(8,128)(2,1)S(1)}, u32[]{:S(2)}, u32[]{:S(2)}) collective-permute-start(bf16[2,144,512]{2,1,0:T(8,128)(2,1)S(1)} %get-tuple-element.55), channel_id=1, source_target_pairs={{0,2},{1,3},{2,0},{3,1},{4,6},{5,7},{6,4},{7,5},{8,10},{9,11},{10,... | collective-permute-start | bytes 884744 | tf_op jit(solution)/shard_map/ppermute | solution.py:35
  30.2 30.1 %collective-permute-start.16 = (bf16[2304,256]{1,0:T(8,128)(2,1)S(1)}, bf16[2304,256]{1,0:T(8,128)(2,1)S(1)}, u32[]{:S(2)}, u32[]{:S(2)}) collective-permute-start(bf16[2304,256]{1,0:T(8,128)(2,1)S(1)} %get-tuple-element.20), channel_id=1, source_target_pairs={{0,4},{1,5},{2,6},{3,7},{4,0},{5,1},{6,2},{7,3},{8,12},{9,13},{10,... | collective-permute-start | bytes 3538952 | tf_op jit(solution)/shard_map/ppermute | solution.py:43
  31.8 8.7 %collective-permute-start.1 = (bf16[2,144,512]{2,1,0:T(8,128)(2,1)S(1)}, bf16[2,144,512]{2,1,0:T(8,128)(2,1)S(1)}, u32[]{:S(2)}, u32[]{:S(2)}) collective-permute-start(bf16[2,144,512]{2,1,0:T(8,128)(2,1)S(1)} %get-tuple-element.55), channel_id=1, source_target_pairs={{0,3},{1,0},{2,1},{3,2},{4,7},{5,4},{6,5},{7,6},{8,11},{9,8},{10,9... | collective-permute-start | bytes 884744 | tf_op jit(solution)/shard_map/ppermute | solution.py:35
  34.6 13.8 %collective-permute-start.10 = (bf16[2,144,512]{2,1,0:T(8,128)(2,1)S(1)}, bf16[2,144,512]{2,1,0:T(8,128)(2,1)S(1)}, u32[]{:S(2)}, u32[]{:S(2)}) collective-permute-start(bf16[2,144,512]{2,1,0:T(8,128)(2,1)S(1)} %get-tuple-element.49), channel_id=1, source_target_pairs={{0,8},{1,9},{2,10},{3,11},{4,12},{5,13},{6,14},{7,15},{8,16},{9,17... | collective-permute-start | bytes 884744 | tf_op jit(solution)/shard_map/ppermute | solution.py:39
  36.2 17.1 %collective-permute-start.9 = (bf16[2,144,512]{2,1,0:T(8,128)(2,1)S(1)}, bf16[2,144,512]{2,1,0:T(8,128)(2,1)S(1)}, u32[]{:S(2)}, u32[]{:S(2)}) collective-permute-start(bf16[2,144,512]{2,1,0:T(8,128)(2,1)S(1)} %get-tuple-element.49), channel_id=1, source_target_pairs={{0,16},{1,17},{2,18},{3,19},{4,20},{5,21},{6,22},{7,23},{8,24},{9,... | collective-permute-start | bytes 884744 | tf_op jit(solution)/shard_map/ppermute | solution.py:39
  39.1 14.2 %collective-permute-start.8 = (bf16[2,144,512]{2,1,0:T(8,128)(2,1)S(1)}, bf16[2,144,512]{2,1,0:T(8,128)(2,1)S(1)}, u32[]{:S(2)}, u32[]{:S(2)}) collective-permute-start(bf16[2,144,512]{2,1,0:T(8,128)(2,1)S(1)} %get-tuple-element.49), channel_id=1, source_target_pairs={{0,24},{1,25},{2,26},{3,27},{4,28},{5,29},{6,30},{7,31},{8,0},{9,1... | collective-permute-start | bytes 884744 | tf_op jit(solution)/shard_map/ppermute | solution.py:39
  40.6 33.6 %collective-permute-start.4 = (bf16[4,2,144,512]{3,2,1,0:T(8,128)(2,1)S(1)}, bf16[4,2,144,512]{3,2,1,0:T(8,128)(2,1)}, u32[]{:S(2)}, u32[]{:S(2)}) collective-permute-start(bf16[4,2,144,512]{3,2,1,0:T(8,128)(2,1)S(1)} %pad_maximum_fusion.refs_4_), channel_id=1, source_target_pairs={{0,8},{1,9},{2,10},{3,11},{4,12},{5,13},{6,14},{7,15},{8,16},{9,17... | collective-permute-start | bytes 3538952 | tf_op jit(solution)/shard_map/ppermute | solution.py:39
  48.4 28.0 %collective-permute-start.5 = (bf16[4,2,144,512]{3,2,1,0:T(8,128)(2,1)S(1)}, bf16[4,2,144,512]{3,2,1,0:T(8,128)(2,1)}, u32[]{:S(2)}, u32[]{:S(2)}) collective-permute-start(bf16[4,2,144,512]{3,2,1,0:T(8,128)(2,1)S(1)} %pad_maximum_fusion.refs_4_), channel_id=1, source_target_pairs={{0,24},{1,25},{2,26},{3,27},{4,28},{5,29},{6,30},{7,31},{8,0},{9,1... | collective-permute-start | bytes 3538952 | tf_op jit(solution)/shard_map/ppermute | solution.py:39
  54.6 25.8 %collective-permute-start.11 = (bf16[4,2,144,512]{3,2,1,0:T(8,128)(2,1)}, bf16[4,2,144,512]{3,2,1,0:T(8,128)(2,1)}, u32[]{:S(2)}, u32[]{:S(2)}) collective-permute-start(bf16[4,2,144,512]{3,2,1,0:T(8,128)(2,1)} %pad_maximum_fusion.1.refs_9_), channel_id=1, source_target_pairs={{0,1},{1,2},{2,3},{3,0},{4,5},{5,6},{6,7},{7,4},{8,9},{9,10},{10,1... | collective-permute-start | bytes 3538952 | tf_op jit(solution)/shard_map/ppermute | solution.py:35
  54.6 30.8 %collective-permute-start.12 = (bf16[4,2,144,512]{3,2,1,0:T(8,128)(2,1)}, bf16[4,2,144,512]{3,2,1,0:T(8,128)(2,1)}, u32[]{:S(2)}, u32[]{:S(2)}) collective-permute-start(bf16[4,2,144,512]{3,2,1,0:T(8,128)(2,1)} %pad_maximum_fusion.1.refs_9_), channel_id=1, source_target_pairs={{0,3},{1,0},{2,1},{3,2},{4,7},{5,4},{6,5},{7,6},{8,11},{9,8},{10,9... | collective-permute-start | bytes 3538952 | tf_op jit(solution)/shard_map/ppermute | solution.py:35
  71.8 15.1 %collective-permute-start.24 = (bf16[2,144,512]{2,1,0:T(8,128)(2,1)}, bf16[2,144,512]{2,1,0:T(8,128)(2,1)}, u32[]{:S(2)}, u32[]{:S(2)}) collective-permute-start(bf16[2,144,512]{2,1,0:T(8,128)(2,1)} %get-tuple-element.38), channel_id=1, source_target_pairs={{0,1},{1,2},{2,3},{3,0},{4,5},{5,6},{6,7},{7,4},{8,9},{9,10},{10,1... | collective-permute-start | bytes 884744 | tf_op jit(solution)/shard_map/ppermute | solution.py:35
  74.3 12.9 %collective-permute-start.26 = (bf16[2,144,512]{2,1,0:T(8,128)(2,1)}, bf16[2,144,512]{2,1,0:T(8,128)(2,1)}, u32[]{:S(2)}, u32[]{:S(2)}) collective-permute-start(bf16[2,144,512]{2,1,0:T(8,128)(2,1)} %get-tuple-element.39), channel_id=1, source_target_pairs={{0,3},{1,0},{2,1},{3,2},{4,7},{5,4},{6,5},{7,6},{8,11},{9,8},{10,9... | collective-permute-start | bytes 884744 | tf_op jit(solution)/shard_map/ppermute | solution.py:35
  76.4 15.0 %collective-permute-start.19 = (bf16[2,144,512]{2,1,0:T(8,128)(2,1)}, bf16[2,144,512]{2,1,0:T(8,128)(2,1)}, u32[]{:S(2)}, u32[]{:S(2)}) collective-permute-start(bf16[2,144,512]{2,1,0:T(8,128)(2,1)} %bitcast.26), channel_id=1, source_target_pairs={{0,24},{1,25},{2,26},{3,27},{4,28},{5,29},{6,30},{7,31},{8,0},{9,1... | collective-permute-start | bytes 884744 | tf_op jit(solution)/shard_map/ppermute | solution.py:39
  80.3 21.2 %collective-permute-start.6 = (bf16[2,2,144,512]{3,2,1,0:T(8,128)(2,1)S(1)}, bf16[2,2,144,512]{3,2,1,0:T(8,128)(2,1)S(1)}, u32[]{:S(2)}, u32[]{:S(2)}) collective-permute-start(bf16[2,2,144,512]{3,2,1,0:T(8,128)(2,1)S(1)} %slice.174), channel_id=1, source_target_pairs={{0,8},{1,9},{2,10},{3,11},{4,12},{5,13},{6,14},{7,15},{8,16},{9,17... | collective-permute-start | bytes 1769480 | tf_op jit(solution)/shard_map/ppermute | solution.py:39
  85.4 17.5 %collective-permute-start.7 = (bf16[2,2,144,512]{3,2,1,0:T(8,128)(2,1)S(1)}, bf16[2,2,144,512]{3,2,1,0:T(8,128)(2,1)S(1)}, u32[]{:S(2)}, u32[]{:S(2)}) collective-permute-start(bf16[2,2,144,512]{3,2,1,0:T(8,128)(2,1)S(1)} %slice.175), channel_id=1, source_target_pairs={{0,24},{1,25},{2,26},{3,27},{4,28},{5,29},{6,30},{7,31},{8,0},{9,1... | collective-permute-start | bytes 1769480 | tf_op jit(solution)/shard_map/ppermute | solution.py:39
  86.9 16.2 %collective-permute-start.13 = (bf16[2,2,144,512]{3,2,1,0:T(8,128)(2,1)S(1)}, bf16[2,2,144,512]{3,2,1,0:T(8,128)(2,1)S(1)}, u32[]{:S(2)}, u32[]{:S(2)}) collective-permute-start(bf16[2,2,144,512]{3,2,1,0:T(8,128)(2,1)S(1)} %slice.178), channel_id=1, source_target_pairs={{0,1},{1,2},{2,3},{3,0},{4,5},{5,6},{6,7},{7,4},{8,9},{9,10},{10,1... | collective-permute-start | bytes 1769480 | tf_op jit(solution)/shard_map/ppermute | solution.py:35
  87.2 17.8 %collective-permute-start.14 = (bf16[2,2,144,512]{3,2,1,0:T(8,128)(2,1)S(1)}, bf16[2,2,144,512]{3,2,1,0:T(8,128)(2,1)S(1)}, u32[]{:S(2)}, u32[]{:S(2)}) collective-permute-start(bf16[2,2,144,512]{3,2,1,0:T(8,128)(2,1)S(1)} %slice.179), channel_id=1, source_target_pairs={{0,3},{1,0},{2,1},{3,2},{4,7},{5,4},{6,5},{7,6},{8,11},{9,8},{10,9... | collective-permute-start | bytes 1769480 | tf_op jit(solution)/shard_map/ppermute | solution.py:35
  91.4 9.2 %collective-permute-start.17 = (bf16[2,144,512]{2,1,0:T(8,128)(2,1)S(1)}, bf16[2,144,512]{2,1,0:T(8,128)(2,1)S(1)}, u32[]{:S(2)}, u32[]{:S(2)}) collective-permute-start(bf16[2,144,512]{2,1,0:T(8,128)(2,1)S(1)} %bitcast.145), channel_id=1, source_target_pairs={{0,8},{1,9},{2,10},{3,11},{4,12},{5,13},{6,14},{7,15},{8,16},{9,17... | collective-permute-start | bytes 884744 | tf_op jit(solution)/shard_map/ppermute | solution.py:39
  100.6 21.8 %collective-permute-start.27 = (bf16[4,144,512]{2,1,0:T(8,128)(2,1)S(1)}, bf16[4,144,512]{2,1,0:T(8,128)(2,1)S(1)}, u32[]{:S(2)}, u32[]{:S(2)}) collective-permute-start(bf16[4,144,512]{2,1,0:T(8,128)(2,1)S(1)} %pad_maximum_fusion.5), channel_id=1, source_target_pairs={{0,3},{1,0},{2,1},{3,2},{4,7},{5,4},{6,5},{7,6},{8,11},{9,8},{10,9... | collective-permute-start | bytes 1769480 | tf_op jit(solution)/shard_map/ppermute | solution.py:35
  101.5 20.9 %collective-permute-start.25 = (bf16[4,144,512]{2,1,0:T(8,128)(2,1)S(1)}, bf16[4,144,512]{2,1,0:T(8,128)(2,1)S(1)}, u32[]{:S(2)}, u32[]{:S(2)}) collective-permute-start(bf16[4,144,512]{2,1,0:T(8,128)(2,1)S(1)} %pad_maximum_fusion.4), channel_id=1, source_target_pairs={{0,1},{1,2},{2,3},{3,0},{4,5},{5,6},{6,7},{7,4},{8,9},{9,10},{10,1... | collective-permute-start | bytes 1769480 | tf_op jit(solution)/shard_map/ppermute | solution.py:35
  102.9 22.7 %collective-permute-start.20 = (bf16[4,144,512]{2,1,0:T(8,128)(2,1)S(1)}, bf16[4,144,512]{2,1,0:T(8,128)(2,1)S(1)}, u32[]{:S(2)}, u32[]{:S(2)}) collective-permute-start(bf16[4,144,512]{2,1,0:T(8,128)(2,1)S(1)} %pad_maximum_fusion.3), channel_id=1, source_target_pairs={{0,24},{1,25},{2,26},{3,27},{4,28},{5,29},{6,30},{7,31},{8,0},{9,1... | collective-permute-start | bytes 1769480 | tf_op jit(solution)/shard_map/ppermute | solution.py:39
  103.0 22.6 %collective-permute-start.18 = (bf16[4,144,512]{2,1,0:T(8,128)(2,1)S(1)}, bf16[4,144,512]{2,1,0:T(8,128)(2,1)S(1)}, u32[]{:S(2)}, u32[]{:S(2)}) collective-permute-start(bf16[4,144,512]{2,1,0:T(8,128)(2,1)S(1)} %pad_maximum_fusion.2), channel_id=1, source_target_pairs={{0,8},{1,9},{2,10},{3,11},{4,12},{5,13},{6,14},{7,15},{8,16},{9,17... | collective-permute-start | bytes 1769480 | tf_op jit(solution)/shard_map/ppermute | solution.py:39
  122.7 6.7 %collective-permute-start.30 = (bf16[144,512]{1,0:T(8,128)(2,1)S(1)}, bf16[144,512]{1,0:T(8,128)(2,1)S(1)}, u32[]{:S(2)}, u32[]{:S(2)}) collective-permute-start(bf16[144,512]{1,0:T(8,128)(2,1)S(1)} %get-tuple-element.46), channel_id=1, source_target_pairs={{0,16},{1,17},{2,18},{3,19},{4,20},{5,21},{6,22},{7,23},{8,24},{9,... | collective-permute-start | bytes 442376 | tf_op jit(solution)/shard_map/ppermute | solution.py:39
  122.9 6.9 %collective-permute-start.29 = (bf16[144,512]{1,0:T(8,128)(2,1)S(1)}, bf16[144,512]{1,0:T(8,128)(2,1)S(1)}, u32[]{:S(2)}, u32[]{:S(2)}) collective-permute-start(bf16[144,512]{1,0:T(8,128)(2,1)S(1)} %get-tuple-element.47), channel_id=1, source_target_pairs={{0,24},{1,25},{2,26},{3,27},{4,28},{5,29},{6,30},{7,31},{8,0},{9,1... | collective-permute-start | bytes 442376 | tf_op jit(solution)/shard_map/ppermute | solution.py:39
  125.6 6.4 %collective-permute-start.28 = (bf16[144,512]{1,0:T(8,128)(2,1)S(1)}, bf16[144,512]{1,0:T(8,128)(2,1)S(1)}, u32[]{:S(2)}, u32[]{:S(2)}) collective-permute-start(bf16[144,512]{1,0:T(8,128)(2,1)S(1)} %get-tuple-element.45), channel_id=1, source_target_pairs={{0,8},{1,9},{2,10},{3,11},{4,12},{5,13},{6,14},{7,15},{8,16},{9,17... | collective-permute-start | bytes 442376 | tf_op jit(solution)/shard_map/ppermute | solution.py:39
  125.9 6.7 %collective-permute-start.23 = (bf16[144,512]{1,0:T(8,128)(2,1)S(1)}, bf16[144,512]{1,0:T(8,128)(2,1)S(1)}, u32[]{:S(2)}, u32[]{:S(2)}) collective-permute-start(bf16[144,512]{1,0:T(8,128)(2,1)S(1)} %get-tuple-element.43), channel_id=1, source_target_pairs={{0,2},{1,3},{2,0},{3,1},{4,6},{5,7},{6,4},{7,5},{8,10},{9,11},{10,... | collective-permute-start | bytes 442376 | tf_op jit(solution)/shard_map/ppermute | solution.py:35
  126.8 6.8 %collective-permute-start.22 = (bf16[144,512]{1,0:T(8,128)(2,1)S(1)}, bf16[144,512]{1,0:T(8,128)(2,1)S(1)}, u32[]{:S(2)}, u32[]{:S(2)}) collective-permute-start(bf16[144,512]{1,0:T(8,128)(2,1)S(1)} %get-tuple-element.44), channel_id=1, source_target_pairs={{0,3},{1,0},{2,1},{3,2},{4,7},{5,4},{6,5},{7,6},{8,11},{9,8},{10,9... | collective-permute-start | bytes 442376 | tf_op jit(solution)/shard_map/ppermute | solution.py:35
  129.5 6.4 %collective-permute-start.21 = (bf16[144,512]{1,0:T(8,128)(2,1)S(1)}, bf16[144,512]{1,0:T(8,128)(2,1)S(1)}, u32[]{:S(2)}, u32[]{:S(2)}) collective-permute-start(bf16[144,512]{1,0:T(8,128)(2,1)S(1)} %get-tuple-element.42), channel_id=1, source_target_pairs={{0,1},{1,2},{2,3},{3,0},{4,5},{5,6},{6,7},{7,4},{8,9},{9,10},{10,1... | collective-permute-start | bytes 442376 | tf_op jit(solution)/shard_map/ppermute | solution.py:35
  (26 other events, 112.6 us)
Sparse Core Ops, SparseCore 0:
  71.9 38.8 all-gather.2
